TPU v7x, 128 devices: a whole 4x4x4 slice. The times are simulated.
128 devices in a mesh: dp: 4 (over x), ctx: 16 (over z, y), head: 2 (over core).
Axes of the slice: x: 4, y: 4, z: 4, core: 2. Of those that a mesh axis runs over, the one named last changes fastest.
Arguments:
- queries: bfloat16 [16384, 32, 128], P(('dp', 'ctx'), 'head'), parts along dimension 0, may hold values from -112 to 112, as said below
- keys: bfloat16 [16384, 16, 128], P(('dp', 'ctx'), 'head'), parts along dimension 0, may hold values from -4 to 4, as said below
- values: bfloat16 [16384, 16, 128], P(('dp', 'ctx'), 'head'), parts along dimension 0, may hold values from -4 to 4
- out_grad: bfloat16 [16384, 32, 128], P(('dp', 'ctx'), 'head'), parts along dimension 0, may hold values from -4 to 4
- doc_lengths: int32 [128], P('dp'), parts along dimension 0, may hold values from 1 to 1024, 4096 in all
Outputs:
- attended: bfloat16 [16384, 32, 128], P(('dp', 'ctx'), 'head'), parts along dimension 0
- query_grad: bfloat16 [16384, 32, 128], P(('dp', 'ctx'), 'head'), parts along dimension 0
- key_grad: bfloat16 [16384, 16, 128], P(('dp', 'ctx'), 'head'), parts along dimension 0
- value_grad: bfloat16 [16384, 16, 128], P(('dp', 'ctx'), 'head'), parts along dimension 0
There are 4 independent parts, one for each index of `dp`. A program takes and returns all parts, laid end to end along the dimension named above; each array names one. Nothing has to cross between parts.
Inputs may be any that keep to these rules, and one draw needn't show every extreme that they name: Entries of the queries lie in this range. Entries of the keys lie in this range. `doc_lengths`: the lengths sum to 4096; the longest document has exactly 1024 tokens.
All inputs are finite; a program needn't handle non-finite values.
Results may differ from a plain program's by a relative error of at most 0.0055.
Values may be sent and summed in bfloat16 or wider, within the bound.
No kernel may reach another device: no remote copies, remote signals or barrier semaphores. Data moves between devices by JAX's collectives and lax.ppermute only.
A program may use at most 192 MiB of HBM per device.

v0:
```python
import functools

import jax
import jax.numpy as jnp
from jax import lax
from jax.experimental import pallas as pl
from jax.experimental.pallas import tpu as pltpu
from jax.sharding import PartitionSpec as P

WINDOW = 1024
SCALING = 168.0 ** (-0.5)
LOG2E = 1.4426950408889634
NEG = -1e30
TILE = 128
VMEM_LIMIT = 48 * 1024 * 1024
HBM = pl.ANY
JOINT = (2, 6)

NT = (((1,), (1,)), ((), ()))
NN = (((1,), (0,)), ((), ()))

VMEM = pl.BlockSpec(memory_space=pltpu.VMEM)
SMEM = pl.BlockSpec(memory_space=pltpu.SMEM)


def dot(a, b, dims):
    return lax.dot_general(a, b, dims, preferred_element_type=jnp.float32)


def place(i, turn, blocks):
    return lax.rem(i + turn, blocks)


def prepare_kernel(meta_ref, kv_ref, halo_ref, k_hbm, kt_hbm, k_ref, kt_ref, k_sem, kt_sem, *, blocks, tile):
    before = halo_ref.shape[0]
    cuts = kv_ref.shape[2] // tile
    turn = meta_ref[1]

    def put(source, index, at):
        for n in range(2):
            for c in range(cuts):
                part = source[index, n, c * tile:(c + 1) * tile]
                k_ref[at * cuts + c, n] = part
                kt_ref[at * cuts + c, n] = part.T

    def halo_step(t, carry):
        put(halo_ref, t, t)
        return carry

    def own_step(t, carry):
        put(kv_ref, place(t, turn, blocks), before + t)
        return carry

    lax.fori_loop(0, before, halo_step, 0)
    lax.fori_loop(0, blocks, own_step, 0, unroll=2)
    copies = [pltpu.make_async_copy(k_ref, k_hbm, k_sem), pltpu.make_async_copy(kt_ref, kt_hbm, kt_sem)]
    for copy in copies:
        copy.start()
    for copy in copies:
        copy.wait()


def prepare(meta, kv, halo, tile):
    blocks, _, rows, dim = kv.shape
    tiles = (halo.shape[0] + blocks) * (rows // tile)
    outs = (
        jax.ShapeDtypeStruct((tiles, 2, tile, dim), kv.dtype),
        jax.ShapeDtypeStruct((tiles, 2, dim, tile), kv.dtype),
    )
    hbm = pl.BlockSpec(memory_space=HBM)
    return pl.pallas_call(
        functools.partial(prepare_kernel, blocks=blocks, tile=tile),
        out_shape=outs,
        in_specs=[SMEM, VMEM, VMEM],
        out_specs=(hbm, hbm),
        scratch_shapes=[pltpu.VMEM(o.shape, o.dtype) for o in outs] + [pltpu.SemaphoreType.DMA] * 2,
        compiler_params=pltpu.CompilerParams(vmem_limit_bytes=12 * 1024 * 1024),
        cost_estimate=pl.CostEstimate(flops=10**6, bytes_accessed=6 * 2**20, transcendentals=0),
    )(meta, kv, halo)


def attention_kernel(
    meta_ref, ends_ref, k_hbm, kt_hbm, x_hbm, y_hbm, acc_hbm, dhalo_hbm,
    k_ref, kt_ref, x_ref, acc_ref, s_ref, g_ref, y_ref, dhalo_ref, k_sem, kt_sem, x_sem, y_sem, acc_sem, dhalo_sem, *, blocks, before, group,
):
    rows, dim = x_ref.shape[2:]
    tile = k_ref.shape[2]
    wide = group * tile
    cuts = rows // tile
    halo = before * cuts
    base, turn = meta_ref[blocks * cuts], meta_ref[blocks * cuts + 1]

    def tile_copies(block):
        near = pl.ds(halo + block * cuts, cuts)
        return [pltpu.make_async_copy(h.at[near], r.at[near], sem.at[block]) for h, r, sem in sources]

    sources = ((k_hbm, k_ref, k_sem), (kt_hbm, kt_ref, kt_sem))
    start_copies = [
        pltpu.make_async_copy(h.at[pl.ds(0, halo + cuts)], r.at[pl.ds(0, halo + cuts)], sem.at[0]) for h, r, sem in sources
    ]

    def x_copy(at):
        return pltpu.make_async_copy(x_hbm.at[at], x_ref.at[at], x_sem.at[at])

    x_copy(place(0, turn, blocks)).start()
    for copy in start_copies:
        copy.start()

    def fetch_step(block, carry):
        x_copy(place(block, turn, blocks)).start()
        for copy in tile_copies(block):
            copy.start()
        return carry

    lax.fori_loop(1, blocks, fetch_step, 0)

    def zero_step(t, carry):
        acc_ref[t] = jnp.zeros(acc_ref.shape[1:], jnp.float32)
        return carry

    lax.fori_loop(0, before, zero_step, 0)

    def acc_at(t, m):
        return t // cuts, m, pl.ds(pl.multiple_of(lax.rem(t, cuts) * tile, tile), tile)

    lane = lax.rem(lax.broadcasted_iota(jnp.int32, (1, wide), 1), tile)
    diff = lane - lax.broadcasted_iota(jnp.int32, (2 * tile, wide), 0)

    def y_copy(at):
        return pltpu.make_async_copy(y_ref.at[at], y_hbm.at[at], y_sem.at[at])

    def acc_copy(t):
        return pltpu.make_async_copy(acc_ref.at[before + t], acc_hbm.at[place(t, turn, blocks)], acc_sem.at[t])

    def dhalo_copy(t):
        return pltpu.make_async_copy(dhalo_ref.at[t], dhalo_hbm.at[t], dhalo_sem.at[t])

    def scores(slot, i, at, piece, count):
        first = halo + i - (count - 1)
        span = pl.ds(piece * tile, tile)
        q = x_ref[at, 0:group, span].reshape(wide, dim)
        do = x_ref[at, group:2 * group, span].reshape(wide, dim)
        pos = base + i * tile + lane
        ends = ends_ref[...]
        start = jnp.max(jnp.where(ends <= pos, ends, 0), axis=0, keepdims=True)
        reach = pos - jnp.maximum(start, pos - (WINDOW - 1))
        chunks = [(0, 1)] * (count % 2) + [(a, 2) for a in range(count % 2, count, 2)]
        top = None
        for a, n in chunks:
            raw = dot(k_ref[pl.ds(first + a, n), 0].reshape(n * tile, dim), q, NT)
            offset = (count - 1 - a) * tile
            keep = diff[:n * tile] <= reach - offset
            if a + n == count:
                keep = keep & (diff[:n * tile] >= -offset)
            raw = jnp.where(keep, raw, NEG)
            s_ref[slot, a * tile:(a + n) * tile] = raw
            here = jnp.max(raw, axis=0, keepdims=True)
            top = here if top is None else jnp.maximum(top, here)
            g_ref[slot, a * tile:(a + n) * tile] = dot(
                k_ref[pl.ds(first + a, n), 1].reshape(n * tile, dim), do, NT
            )
        return first, q, do, chunks, top

    def weigh(slot, state):
        first, q, do, chunks, top = state
        total = mixed = 0.0
        for a, n in chunks:
            p = jnp.exp2((s_ref[slot, a * tile:(a + n) * tile] - top) * (SCALING * LOG2E))
            s_ref[slot, a * tile:(a + n) * tile] = p
            total += jnp.sum(p, axis=0, keepdims=True)
            mixed += jnp.sum(p * g_ref[slot, a * tile:(a + n) * tile], axis=0, keepdims=True)
        inverse = 1.0 / total
        return first, q, do, chunks, inverse, mixed * inverse

    def gradients(slot, at, piece, count, state):
        first, q, do, chunks, inverse, row_total = state
        span = pl.ds(piece * tile, tile)
        out = dq = 0.0
        for a, n in chunks:
            w = s_ref[slot, a * tile:(a + n) * tile] * inverse
            wb = w.astype(jnp.bfloat16)
            ds = (w * (g_ref[slot, a * tile:(a + n) * tile] - row_total)).astype(jnp.bfloat16)
            kt, vt = (
                jnp.concatenate([kt_ref[first + a + c, m] for c in range(n)], axis=1) for m in range(2)
            )
            out += dot(vt, wb, NN)
            dq += dot(kt, ds, NN)
            for m, part in enumerate((dot(ds, q, NN), dot(wb, do, NN))):
                for c in range(n):
                    here = acc_at(first + a + c, m)
                    if a + c == count - 1:
                        acc_ref[here] = part[c * tile:]
                    else:
                        acc_ref[here] += part[c * tile:(c + 1) * tile]
        y_ref[at, 0:group, span] = out.T.astype(jnp.bfloat16).reshape(group, tile, dim)
        y_ref[at, group:2 * group, span] = (SCALING * dq).T.astype(jnp.bfloat16).reshape(group, tile, dim)

    def query_tiles(block, at, pieces, count):
        states = [scores(slot, block * cuts + c, at, c, count) for slot, c in enumerate(pieces)]
        states = [weigh(slot, state) for slot, state in enumerate(states)]
        for slot, c in enumerate(pieces):
            gradients(slot, at, c, count, states[slot])

    def block_step(block, carry):
        at = place(block, turn, blocks)
        counts = [meta_ref[block * cuts + c] for c in range(cuts)]
        most = functools.reduce(jnp.maximum, counts)
        x_copy(at).wait()

        @pl.when(block == 0)
        def _():
            for copy in start_copies:
                copy.wait()

        @pl.when(block > 0)
        def _():
            for copy in tile_copies(block):
                copy.wait()

        for n in range(JOINT[0], JOINT[1]):
            here = (most == n) if n > JOINT[0] else (most <= n)
            pl.when(here)(functools.partial(query_tiles, block, at, list(range(cuts)), n))
        for c in range(cuts):
            for n in range(1, halo + 2):
                here = (counts[c] == n) & (most >= JOINT[1])
                pl.when(here)(functools.partial(query_tiles, block, at, [c], n))
        y_copy(at).start()

        @pl.when(block < before)
        def _():
            dhalo_ref[block, 0] = (SCALING * acc_ref[block, 0]).astype(jnp.bfloat16)
            dhalo_ref[block, 1] = acc_ref[block, 1].astype(jnp.bfloat16)
            dhalo_copy(block).start()

        @pl.when(block >= before)
        def _():
            acc_copy(block - before).start()

        return carry

    lax.fori_loop(0, blocks, block_step, 0)
    for t in range(blocks - before, blocks):
        acc_copy(t).start()

    def wait_step(i, carry):
        y_copy(i).wait()
        acc_copy(i).wait()
        return carry

    def halo_wait_step(t, carry):
        dhalo_copy(t).wait()
        return carry

    lax.fori_loop(0, blocks, wait_step, 0)
    lax.fori_loop(0, before, halo_wait_step, 0)


def attention(meta, ends, k, kt, x, before):
    blocks, _, rows, dim = x.shape
    group = x.shape[1] // 2
    tiles, _, tile, _ = k.shape
    cuts = rows // tile
    hbm = pl.BlockSpec(memory_space=HBM)
    any_space = pl.BlockSpec(memory_space=pl.ANY)
    most = before * cuts + 1
    return pl.pallas_call(
        functools.partial(attention_kernel, blocks=blocks, before=before, group=group),
        out_shape=(
            jax.ShapeDtypeStruct(x.shape, jnp.bfloat16),
            jax.ShapeDtypeStruct((blocks, 2, rows, dim), jnp.float32),
            jax.ShapeDtypeStruct((before, 2, rows, dim), jnp.bfloat16),
        ),
        in_specs=[SMEM, VMEM, any_space, any_space, any_space],
        out_specs=(any_space, any_space, any_space),
        scratch_shapes=[
            pltpu.VMEM(k.shape, k.dtype),
            pltpu.VMEM(kt.shape, kt.dtype),
            pltpu.VMEM(x.shape, x.dtype),
            pltpu.VMEM((before + blocks, 2, rows, dim), jnp.float32),
            pltpu.VMEM((cuts, most * tile, group * tile), jnp.float32),
            pltpu.VMEM((cuts, most * tile, group * tile), jnp.float32),
            pltpu.VMEM(x.shape, jnp.bfloat16),
            pltpu.VMEM((before, 2, rows, dim), jnp.bfloat16),
            pltpu.SemaphoreType.DMA((blocks,)),
            pltpu.SemaphoreType.DMA((blocks,)),
            pltpu.SemaphoreType.DMA((blocks,)),
            pltpu.SemaphoreType.DMA((blocks,)),
            pltpu.SemaphoreType.DMA((blocks,)),
            pltpu.SemaphoreType.DMA((before,)),
        ],
        compiler_params=pltpu.CompilerParams(vmem_limit_bytes=VMEM_LIMIT),
        cost_estimate=pl.CostEstimate(flops=5 * 10**9, bytes_accessed=12 * 2**20, transcendentals=4 * 10**6),
    )(meta, ends, k, kt, x)


def gather_kernel(k_ref, v_ref, out_ref):
    out_ref[:, 0] = jnp.swapaxes(k_ref[...], 0, 1)
    out_ref[:, 1] = jnp.swapaxes(v_ref[...], 0, 1)


def gather_heads(k, v, part):
    rows, heads, dim = k.shape
    return pl.pallas_call(
        gather_kernel,
        grid=(rows // part,),
        out_shape=jax.ShapeDtypeStruct((heads, 2, rows, dim), k.dtype),
        in_specs=[pl.BlockSpec((part, heads, dim), lambda i: (i, 0, 0))] * 2,
        out_specs=pl.BlockSpec((heads, 2, part, dim), lambda i: (0, 0, i, 0)),
        cost_estimate=pl.CostEstimate(flops=10**6, bytes_accessed=2 * 2**20, transcendentals=0),
    )(k, v)


def scatter_kernel(x_ref, k_ref, v_ref):
    k_ref[...] = jnp.swapaxes(x_ref[:, 0], 0, 1)
    v_ref[...] = jnp.swapaxes(x_ref[:, 1], 0, 1)


def scatter_heads(x, part):
    heads, _, rows, dim = x.shape
    one = jax.ShapeDtypeStruct((rows, heads, dim), x.dtype)
    return pl.pallas_call(
        scatter_kernel,
        grid=(rows // part,),
        out_shape=(one, one),
        in_specs=[pl.BlockSpec((heads, 2, part, dim), lambda i: (0, 0, i, 0))],
        out_specs=(pl.BlockSpec((part, heads, dim), lambda i: (i, 0, 0)),) * 2,
        cost_estimate=pl.CostEstimate(flops=10**6, bytes_accessed=2 * 2**20, transcendentals=0),
    )(x)


def after(array, other):
    return lax.optimization_barrier((array, other))[0]


def body(queries, keys, values, out_grad, doc_lengths):
    rows, heads, dim = queries.shape
    kv_heads = keys.shape[1]
    group = heads // kv_heads
    blocks = kv_heads
    parts = lax.axis_size("ctx") // blocks
    before = WINDOW // rows
    tile = TILE
    turns = [(p % 2) * (blocks // 2) for p in range(parts)]
    groups = [[p * blocks + (r + turns[p]) % blocks for r in range(blocks)] for p in range(parts)]
    onward = [(groups[p][r], groups[p + 1][r]) for p in range(parts - 1) for r in range(blocks)]
    part = lax.axis_index("ctx") // blocks

    docs = doc_lengths.shape[0]
    upto = jnp.arange(docs)[:, None] >= jnp.arange(docs)[None, :]
    ends = jnp.sum(jnp.where(upto, doc_lengths[None, :], 0), axis=1)
    base = part * blocks * rows
    turn = lax.rem(part, 2) * (blocks // 2)
    position = base + jnp.arange(blocks * (rows // tile), dtype=jnp.int32) * tile
    start = jnp.max(jnp.where(ends[None, :] <= position[:, None], ends[None, :], 0), axis=1)
    first = jnp.maximum(jnp.maximum(start, position - (WINDOW - 1)), 0)
    meta = jnp.concatenate((position // tile - first // tile + 1, jnp.stack((base, turn)))).astype(jnp.int32)
    ends = ends[:, None].astype(jnp.int32)

    def exchange(array):
        return lax.all_to_all(array, "ctx", 0, 0, axis_index_groups=groups)

    def by_head(array):
        array = jnp.swapaxes(array, 0, 1)
        return array.reshape(kv_heads, array.shape[0] // kv_heads, array.shape[1], dim)

    def by_token(array):
        array = array.reshape(array.shape[0] * array.shape[1], array.shape[2], dim)
        return jnp.swapaxes(array, 0, 1)

    kv = exchange(gather_heads(keys, values, TILE))
    tail = jnp.stack([kv[(blocks - before + t + turns[0]) % blocks] for t in range(before)]) if turns[0] else kv[blocks - before:]
    halo = lax.ppermute(tail, "ctx", onward)
    packed = jnp.concatenate([by_head(a) for a in (queries, out_grad)], 1)
    x = exchange(after(packed, kv))
    k, kt = prepare(jnp.stack((base, turn)).astype(jnp.int32), kv, halo, tile)
    y, dkv, dhalo = attention(meta, ends, k, kt, x, before)
    dhalo = lax.ppermute(dhalo, "ctx", [(b, a) for a, b in onward])
    y = exchange(y)
    factor = jnp.where(jnp.arange(2) == 0, SCALING, 1.0).astype(jnp.float32)[:, None, None]
    dhalo = jnp.pad(dhalo.astype(jnp.float32), ((blocks - before, 0), (0, 0), (0, 0), (0, 0)))
    dkv = (dkv * factor + dhalo).astype(jnp.bfloat16)
    dkv = exchange(after(dkv, y))
    dk, dv = scatter_heads(dkv, TILE)
    return by_token(y[:, :group]), by_token(y[:, group:]), dk, dv


def solution(mesh):
    spec = P(("dp", "ctx"), "head", None)
    return jax.shard_map(
        body,
        mesh=mesh,
        in_specs=(spec, spec, spec, spec, P("dp")),
        out_specs=(spec, spec, spec, spec),
        check_vma=False,
    )
```

profile of v0, /device:TPU:1, one launch (start us, length us, event | category | flops | bytes accessed | tf_op | source)
XLA Modules:
  0.0 128.8 jit_solution(18348869074300647367)
XLA Ops:
  0.6 0.0 copy-start.2
  0.6 2.2 %shard_map.84 = bf16[8,2,256,128]{3,2,1,0:T(8,128)(2,1)} custom-call(bf16[256,8,128]{2,1,0:T(8,128)(2,1)} %k_ref.1, bf16[256,8,128]{2,1,0:T(8,128)(2,1)} %v_ref.1), custom_call_target="tpu_custom_call" | custom-call | flops 1000000 | bytes 2097152 | tf_op jit(solution)/shard_map/pallas_call | solution.py:303
  2.8 0.0 copy-start.3
  2.8 6.5 %all-to-all-start = ((bf16[8,2,256,128]{3,2,1,0:T(8,128)(2,1)}), bf16[8,2,256,128]{3,2,1,0:T(8,128)(2,1)S(1)}, u32[]{:S(2)}, u32[]{:S(2)}) async-start(bf16[8,2,256,128]{3,2,1,0:T(8,128)(2,1)} %shard_map.84), calls=%async_computation | async-start | bytes 2097152 | tf_op jit(solution)/shard_map/all_to_all | solution.py:360
  9.3 0.0 copy-done.2
  9.3 0.3 copy.14
  9.6 0.0 copy-done.3
  9.6 0.3 copy.15
  9.9 1.5 %pad_maximum_fusion = bf16[8,4,256,128]{3,2,1,0:T(8,128)(2,1)} fusion(bf16[8,2,256,128]{3,2,1,0:T(8,128)(2,1)S(1)} %bitcast.14, bf16[8,2,256,128]{3,2,1,0:T(8,128)(2,1)S(1)} %bitcast.13), kind=kLoop, calls=%fused_computation | loop fusion | flops 1048576 | bytes 4194304 | tf_op jit(solution)/shard_map/concatenate | solution.py:373
  11.4 0.0 copy-start.4
  11.4 13.7 %all-to-all-done.kv_ref = bf16[8,2,256,128]{3,2,1,0:T(8,128)(2,1)S(1)} async-done(((bf16[8,2,256,128]{3,2,1,0:T(8,128)(2,1)}), bf16[8,2,256,128]{3,2,1,0:T(8,128)(2,1)S(1)}, u32[]{:S(2)}, u32[]{:S(2)}) %all-to-all-start) | async-done | bytes 1048608 | tf_op jit(solution)/shard_map/all_to_all | solution.py:360
  25.1 4.4 %all-to-all-start.1 = ((bf16[8,4,256,128]{3,2,1,0:T(8,128)(2,1)}), bf16[8,4,256,128]{3,2,1,0:T(8,128)(2,1)}, u32[]{:S(2)}, u32[]{:S(2)}) async-start(bf16[8,4,256,128]{3,2,1,0:T(8,128)(2,1)} %pad_maximum_fusion), calls=%async_computation.1 | async-start | bytes 4194304 | tf_op jit(solution)/shard_map/all_to_all | solution.py:360
  29.5 0.0 copy-done.4
  29.5 0.1 select_reduce_fusion
  29.6 0.1 copy.16.ends_ref
  29.8 4.3 %collective-permute-start = (bf16[4,2,256,128]{3,2,1,0:T(8,128)(2,1)S(1)}, bf16[4,2,256,128]{3,2,1,0:T(8,128)(2,1)S(1)}, u32[]{:S(2)}, u32[]{:S(2)}) collective-permute-start(bf16[4,2,256,128]{3,2,1,0:T(8,128)(2,1)S(1)} %slice.12), channel_id=1, source_target_pairs={{0,24},{2,26},{4,28},{6,30},{8,16},{10,18},{12,20},{14,22},{1,25},... | collective-permute-start | bytes 1572872 | tf_op jit(solution)/shard_map/ppermute | solution.py:372
  34.1 0.1 pad_add_fusion.1.meta_ref
  34.2 0.2 select_reduce_fusion.1
  34.4 0.1 pad_add_fusion.meta_ref
  34.5 10.0 %collective-permute-done.halo_ref = bf16[4,2,256,128]{3,2,1,0:T(8,128)(2,1)S(1)} collective-permute-done((bf16[4,2,256,128]{3,2,1,0:T(8,128)(2,1)S(1)}, bf16[4,2,256,128]{3,2,1,0:T(8,128)(2,1)S(1)}, u32[]{:S(2)}, u32[]{:S(2)}) %collective-permute-start) | collective-permute-done | bytes 524320 | tf_op jit(solution)/shard_map/ppermute | solution.py:372
  44.5 1.7 %shard_map.85 = (bf16[24,2,128,128]{3,2,1,0:T(8,128)(2,1)S(1)}, bf16[24,2,128,128]{3,2,1,0:T(8,128)(2,1)S(1)}) custom-call(s32[2]{0:T(128)S(1)} %pad_add_fusion.1.meta_ref, bf16[8,2,256,128]{3,2,1,0:T(8,128)(2,1)S(1)} %all-to-all-done.kv_ref, bf16[4,2,256,128]{3,2,1,0:T(8,128)(2,1)S(1)} %collective-permute-done.halo_ref), custom_call_target="tpu_custom_call" | custom-call | flops 1000000 | bytes 6291456 | tf_op jit(solution)/shard_map/pallas_call | solution.py:71
  46.2 0.0 copy-start
  46.2 1.2 copy-done
  47.4 9.2 %all-to-all-done.1.x_hbm = bf16[8,4,256,128]{3,2,1,0:T(8,128)(2,1)} async-done(((bf16[8,4,256,128]{3,2,1,0:T(8,128)(2,1)}), bf16[8,4,256,128]{3,2,1,0:T(8,128)(2,1)}, u32[]{:S(2)}, u32[]{:S(2)}) %all-to-all-start.1) | async-done | bytes 2097184 | tf_op jit(solution)/shard_map/all_to_all | solution.py:360
  56.6 0.0 copy-start.1
  56.6 1.4 %copy-done.1 = bf16[24,2,128,128]{3,2,1,0:T(8,128)(2,1)S(1)} copy-done((bf16[24,2,128,128]{3,2,1,0:T(8,128)(2,1)S(1)}, bf16[24,2,128,128]{3,2,1,0:T(8,128)(2,1)}, u32[]{:S(2)}) %copy-start.1) | copy-done | bytes 1572888
  58.0 16.6 %shard_map.86 = (bf16[8,4,256,128]{3,2,1,0:T(8,128)(2,1)}, f32[8,2,256,128]{3,2,1,0:T(8,128)}, bf16[4,2,256,128]{3,2,1,0:T(8,128)(2,1)S(1)}) custom-call(s32[18]{0:T(128)S(1)} %pad_add_fusion.meta_ref, s32[32,1]{1,0:T(8,128)S(1)} %copy.16.ends_ref, bf16[24,2,128,128]{3,2,1,0:T(8,128)(2,1)S(1)} %get-tuple-element.13.k_hbm, ...), custom_call_target="tpu_custom_call" | custom-call | flops 5000000000 | bytes 12582912 | tf_op jit(solution)/shard_map/pallas_call | solution.py:266
  74.6 5.1 %all-to-all-start.2 = ((bf16[8,4,256,128]{3,2,1,0:T(8,128)(2,1)}), bf16[8,4,256,128]{3,2,1,0:T(8,128)(2,1)S(1)}, u32[]{:S(2)}, u32[]{:S(2)}) async-start(bf16[8,4,256,128]{3,2,1,0:T(8,128)(2,1)} %get-tuple-element.16), calls=%async_computation.2 | async-start | bytes 4194304 | tf_op jit(solution)/shard_map/all_to_all | solution.py:360
  79.7 1.3 collective-permute-start.1
  81.0 13.1 %collective-permute-done.1 = bf16[4,2,256,128]{3,2,1,0:T(8,128)(2,1)S(1)} collective-permute-done((bf16[4,2,256,128]{3,2,1,0:T(8,128)(2,1)S(1)}, bf16[4,2,256,128]{3,2,1,0:T(8,128)(2,1)S(1)}, u32[]{:S(2)}, u32[]{:S(2)}) %collective-permute-start.1) | collective-permute-done | bytes 524320 | tf_op jit(solution)/shard_map/ppermute | solution.py:377
  94.1 2.9 %add_convert_fusion = bf16[8,2,256,128]{3,2,1,0:T(8,128)(2,1)} fusion(f32[8,2,256,128]{3,2,1,0:T(8,128)} %get-tuple-element.17, bf16[4,2,256,128]{3,2,1,0:T(8,128)(2,1)S(1)} %collective-permute-done.1, f32[2]{0:T(128)S(1)} %compare_select_fusion), kind=kLoop, calls=%fused_computation.1 | loop fusion | flops 2097152 | bytes 3670024 | tf_op jit(solution)/shard_map/convert_element_type | solution.py:381
  97.0 9.7 %all-to-all-done.2 = bf16[8,4,256,128]{3,2,1,0:T(8,128)(2,1)S(1)} async-done(((bf16[8,4,256,128]{3,2,1,0:T(8,128)(2,1)}), bf16[8,4,256,128]{3,2,1,0:T(8,128)(2,1)S(1)}, u32[]{:S(2)}, u32[]{:S(2)}) %all-to-all-start.2) | async-done | bytes 2097184 | tf_op jit(solution)/shard_map/all_to_all | solution.py:360
  106.7 4.2 %all-to-all-start.3 = ((bf16[8,2,256,128]{3,2,1,0:T(8,128)(2,1)}), bf16[8,2,256,128]{3,2,1,0:T(8,128)(2,1)}, u32[]{:S(2)}, u32[]{:S(2)}) async-start(bf16[8,2,256,128]{3,2,1,0:T(8,128)(2,1)} %add_convert_fusion), calls=%async_computation.3 | async-start | bytes 2097152 | tf_op jit(solution)/shard_map/all_to_all | solution.py:360
  111.0 0.2 fusion
  111.1 2.7 %copy_bitcast_fusion = (bf16[256,16,128]{2,1,0:T(8,128)(2,1)}, bf16[256,16,128]{2,1,0:T(8,128)(2,1)}) fusion(bf16[16,256,128]{2,1,0:T(8,128)(2,1)S(1)} %bitcast.15, bf16[16,256,128]{2,1,0:T(8,128)(2,1)S(1)} %bitcast.16), kind=kLoop, calls=%fused_computation.2 | loop fusion | bytes 4194304 | tf_op jit(solution)/shard_map/transpose | solution.py:368
  113.8 13.0 %all-to-all-done.3.x_ref = bf16[8,2,256,128]{3,2,1,0:T(8,128)(2,1)} async-done(((bf16[8,2,256,128]{3,2,1,0:T(8,128)(2,1)}), bf16[8,2,256,128]{3,2,1,0:T(8,128)(2,1)}, u32[]{:S(2)}, u32[]{:S(2)}) %all-to-all-start.3) | async-done | bytes 1048608 | tf_op jit(solution)/shard_map/all_to_all | solution.py:360
  126.8 2.0 %shard_map.87 = (bf16[256,8,128]{2,1,0:T(8,128)(2,1)}, bf16[256,8,128]{2,1,0:T(8,128)(2,1)}) custom-call(bf16[8,2,256,128]{3,2,1,0:T(8,128)(2,1)} %all-to-all-done.3.x_ref), custom_call_target="tpu_custom_call" | custom-call | flops 1000000 | bytes 2097152 | tf_op jit(solution)/shard_map/pallas_call | solution.py:321
  (4 shorter events, 0.1 us)
Async XLA Ops:
  0.6 8.7 %copy-start.2 = (bf16[256,16,128]{2,1,0:T(8,128)(2,1)S(1)}, bf16[256,16,128]{2,1,0:T(8,128)(2,1)}, u32[]{:S(2)}) copy-start(bf16[256,16,128]{2,1,0:T(8,128)(2,1)} %param.5) | copy-start | bytes 3145732
  2.8 6.8 %copy-start.3 = (bf16[256,16,128]{2,1,0:T(8,128)(2,1)S(1)}, bf16[256,16,128]{2,1,0:T(8,128)(2,1)}, u32[]{:S(2)}) copy-start(bf16[256,16,128]{2,1,0:T(8,128)(2,1)} %param.8) | copy-start | bytes 3145732
  2.8 22.3 %all-to-all-start = ((bf16[8,2,256,128]{3,2,1,0:T(8,128)(2,1)}), bf16[8,2,256,128]{3,2,1,0:T(8,128)(2,1)S(1)}, u32[]{:S(2)}, u32[]{:S(2)}) async-start(bf16[8,2,256,128]{3,2,1,0:T(8,128)(2,1)} %shard_map.84), calls=%async_computation | async-start | bytes 2097152 | tf_op jit(solution)/shard_map/all_to_all | solution.py:360
  11.4 18.1 %copy-start.4 = (s32[32]{0:T(128)S(1)}, s32[32]{0:T(128)}, u32[]{:S(2)}) copy-start(s32[32]{0:T(128)} %param.9) | copy-start | bytes 388
  25.1 31.4 %all-to-all-start.1 = ((bf16[8,4,256,128]{3,2,1,0:T(8,128)(2,1)}), bf16[8,4,256,128]{3,2,1,0:T(8,128)(2,1)}, u32[]{:S(2)}, u32[]{:S(2)}) async-start(bf16[8,4,256,128]{3,2,1,0:T(8,128)(2,1)} %pad_maximum_fusion), calls=%async_computation.1 | async-start | bytes 4194304 | tf_op jit(solution)/shard_map/all_to_all | solution.py:360
  29.8 14.7 %collective-permute-start = (bf16[4,2,256,128]{3,2,1,0:T(8,128)(2,1)S(1)}, bf16[4,2,256,128]{3,2,1,0:T(8,128)(2,1)S(1)}, u32[]{:S(2)}, u32[]{:S(2)}) collective-permute-start(bf16[4,2,256,128]{3,2,1,0:T(8,128)(2,1)S(1)} %slice.12), channel_id=1, source_target_pairs={{0,24},{2,26},{4,28},{6,30},{8,16},{10,18},{12,20},{14,22},{1,25},... | collective-permute-start | bytes 1572872 | tf_op jit(solution)/shard_map/ppermute | solution.py:372
  46.2 1.2 copy-start
  56.6 1.4 %copy-start.1 = (bf16[24,2,128,128]{3,2,1,0:T(8,128)(2,1)S(1)}, bf16[24,2,128,128]{3,2,1,0:T(8,128)(2,1)}, u32[]{:S(2)}) copy-start(bf16[24,2,128,128]{3,2,1,0:T(8,128)(2,1)} %copy-done) | copy-start | bytes 4718596
  74.6 32.1 %all-to-all-start.2 = ((bf16[8,4,256,128]{3,2,1,0:T(8,128)(2,1)}), bf16[8,4,256,128]{3,2,1,0:T(8,128)(2,1)S(1)}, u32[]{:S(2)}, u32[]{:S(2)}) async-start(bf16[8,4,256,128]{3,2,1,0:T(8,128)(2,1)} %get-tuple-element.16), calls=%async_computation.2 | async-start | bytes 4194304 | tf_op jit(solution)/shard_map/all_to_all | solution.py:360
  79.7 14.4 %collective-permute-start.1 = (bf16[4,2,256,128]{3,2,1,0:T(8,128)(2,1)S(1)}, bf16[4,2,256,128]{3,2,1,0:T(8,128)(2,1)S(1)}, u32[]{:S(2)}, u32[]{:S(2)}) collective-permute-start(bf16[4,2,256,128]{3,2,1,0:T(8,128)(2,1)S(1)} %get-tuple-element.18), channel_id=1, source_target_pairs={{24,0},{26,2},{28,4},{30,6},{16,8},{18,10},{20,12},{22,14},{25,1},... | collective-permute-start | bytes 1572872 | tf_op jit(solution)/shard_map/ppermute | solution.py:377
  106.7 20.1 %all-to-all-start.3 = ((bf16[8,2,256,128]{3,2,1,0:T(8,128)(2,1)}), bf16[8,2,256,128]{3,2,1,0:T(8,128)(2,1)}, u32[]{:S(2)}, u32[]{:S(2)}) async-start(bf16[8,2,256,128]{3,2,1,0:T(8,128)(2,1)} %add_convert_fusion), calls=%async_computation.3 | async-start | bytes 2097152 | tf_op jit(solution)/shard_map/all_to_all | solution.py:360
where the time goes:
time: 130 us; the launch traced here: 129 us
  waiting for transfers between devices  68.8 us (53%)
  starting transfers between devices  25.8 us (20%)
  Pallas kernels  22.5 us (17%)
  local copies, waits for them, and re-layouts  6.09 us (5%)
  other arithmetic  4.87 us (4%)
    all_to_all x4, waiting for transfers between devices, exchange(): return lax.all_to_all(array, 'ctx', 0, 0, axis_index_groups=groups)  45.6 us
    all_to_all x4, starting transfers between devices, exchange(): return lax.all_to_all(array, 'ctx', 0, 0, axis_index_groups=groups)  20.2 us
    pallas_call x1, Pallas kernels, attention(): pl.pallas_call(functools.partial(attention_kernel, blocks=blocks, before=...  16.6 us
    ppermute x1, waiting for transfers between devices, body(): dhalo = lax.ppermute(dhalo, 'ctx', [(b, a) for a, b in onward])  13.1 us
    ppermute x1, waiting for transfers between devices, body(): halo = lax.ppermute(tail, 'ctx', onward)  9.99 us
    ppermute x1, starting transfers between devices, body(): halo = lax.ppermute(tail, 'ctx', onward)  4.34 us
    convert_element_type x1, other arithmetic, body(): dkv = (dkv * factor + dhalo).astype(jnp.bfloat16)  2.89 us
    transpose x1, local copies, waits for them, and re-layouts, by_token(): return jnp.swapaxes(array, 0, 1)  2.67 us
  transfers between devices with their start and end apart: 6, of which 6 were waited for; matrix products, arithmetic and copies ran while one was open for 6% of the time, Pallas kernels for 1%

commit v1 on v0

--- a/solution.py
+++ b/solution.py
@@ -14,7 +14,7 @@
 TILE = 128
 VMEM_LIMIT = 48 * 1024 * 1024
 HBM = pl.ANY
-JOINT = (2, 6)
+JOINT = (2, 8)
 
 NT = (((1,), (1,)), ((), ()))
 NN = (((1,), (0,)), ((), ()))

time: 130 us -> 130 us (level)
  the two profiles are of different devices: /device:TPU:1 before, /device:TPU:2 now
where the time goes in v1:
time: 130 us
  waiting for transfers between devices  67.1 us (52%)
  starting transfers between devices  26.8 us (21%)
  Pallas kernels  24.1 us (19%)
  local copies, waits for them, and re-layouts  6.09 us (5%)
  other arithmetic  4.87 us (4%)
    all_to_all x4, waiting for transfers between devices, exchange(): return lax.all_to_all(array, 'ctx', 0, 0, axis_index_groups=groups)  42.5 us
    all_to_all x4, starting transfers between devices, exchange(): return lax.all_to_all(array, 'ctx', 0, 0, axis_index_groups=groups)  20.9 us
    pallas_call x1, Pallas kernels, attention(): pl.pallas_call(functools.partial(attention_kernel, blocks=blocks, before=...  18.2 us
    ppermute x1, waiting for transfers between devices, body(): dhalo = lax.ppermute(dhalo, 'ctx', [(b, a) for a, b in onward])  14.1 us
    ppermute x1, waiting for transfers between devices, body(): halo = lax.ppermute(tail, 'ctx', onward)  10.6 us
    ppermute x1, starting transfers between devices, body(): halo = lax.ppermute(tail, 'ctx', onward)  4.62 us
    convert_element_type x1, other arithmetic, body(): dkv = (dkv * factor + dhalo).astype(jnp.bfloat16)  2.89 us
    transpose x1, local copies, waits for them, and re-layouts, by_token(): return jnp.swapaxes(array, 0, 1)  2.67 us
  transfers between devices with their start and end apart: 6, of which 6 were waited for; matrix products, arithmetic and copies ran while one was open for 6% of the time, Pallas kernels for 1%

profile of v1, /device:TPU:2, one launch (start us, length us, event | category | flops | bytes accessed | tf_op | source)
XLA Modules:
  0.0 129.8 jit_solution(1874327641387787313)
XLA Ops:
  0.6 0.0 copy-start.2
  0.6 2.2 %shard_map.84 = bf16[8,2,256,128]{3,2,1,0:T(8,128)(2,1)} custom-call(bf16[256,8,128]{2,1,0:T(8,128)(2,1)} %k_ref.1, bf16[256,8,128]{2,1,0:T(8,128)(2,1)} %v_ref.1), custom_call_target="tpu_custom_call" | custom-call | flops 1000000 | bytes 2097152 | tf_op jit(solution)/shard_map/pallas_call | solution.py:303
  2.8 0.0 copy-start.3
  2.8 6.0 %all-to-all-start = ((bf16[8,2,256,128]{3,2,1,0:T(8,128)(2,1)}), bf16[8,2,256,128]{3,2,1,0:T(8,128)(2,1)S(1)}, u32[]{:S(2)}, u32[]{:S(2)}) async-start(bf16[8,2,256,128]{3,2,1,0:T(8,128)(2,1)} %shard_map.84), calls=%async_computation | async-start | bytes 2097152 | tf_op jit(solution)/shard_map/all_to_all | solution.py:360
  8.8 0.0 copy-done.2
  8.8 0.3 copy.14
  9.1 0.0 copy-done.3
  9.1 0.3 copy.15
  9.3 1.5 %pad_maximum_fusion = bf16[8,4,256,128]{3,2,1,0:T(8,128)(2,1)} fusion(bf16[8,2,256,128]{3,2,1,0:T(8,128)(2,1)S(1)} %bitcast.14, bf16[8,2,256,128]{3,2,1,0:T(8,128)(2,1)S(1)} %bitcast.13), kind=kLoop, calls=%fused_computation | loop fusion | flops 1048576 | bytes 4194304 | tf_op jit(solution)/shard_map/concatenate | solution.py:373
  10.8 0.0 copy-start.4
  10.9 13.6 %all-to-all-done.kv_ref = bf16[8,2,256,128]{3,2,1,0:T(8,128)(2,1)S(1)} async-done(((bf16[8,2,256,128]{3,2,1,0:T(8,128)(2,1)}), bf16[8,2,256,128]{3,2,1,0:T(8,128)(2,1)S(1)}, u32[]{:S(2)}, u32[]{:S(2)}) %all-to-all-start) | async-done | bytes 1048608 | tf_op jit(solution)/shard_map/all_to_all | solution.py:360
  24.5 4.4 %all-to-all-start.1 = ((bf16[8,4,256,128]{3,2,1,0:T(8,128)(2,1)}), bf16[8,4,256,128]{3,2,1,0:T(8,128)(2,1)}, u32[]{:S(2)}, u32[]{:S(2)}) async-start(bf16[8,4,256,128]{3,2,1,0:T(8,128)(2,1)} %pad_maximum_fusion), calls=%async_computation.1 | async-start | bytes 4194304 | tf_op jit(solution)/shard_map/all_to_all | solution.py:360
  28.9 0.0 copy-done.4
  28.9 0.1 select_reduce_fusion
  29.0 0.1 copy.16.ends_ref
  29.1 4.6 %collective-permute-start = (bf16[4,2,256,128]{3,2,1,0:T(8,128)(2,1)S(1)}, bf16[4,2,256,128]{3,2,1,0:T(8,128)(2,1)S(1)}, u32[]{:S(2)}, u32[]{:S(2)}) collective-permute-start(bf16[4,2,256,128]{3,2,1,0:T(8,128)(2,1)S(1)} %slice.12), channel_id=1, source_target_pairs={{0,24},{2,26},{4,28},{6,30},{8,16},{10,18},{12,20},{14,22},{1,25},... | collective-permute-start | bytes 1572872 | tf_op jit(solution)/shard_map/ppermute | solution.py:372
  33.7 0.1 pad_add_fusion.1.meta_ref
  33.8 0.2 select_reduce_fusion.1
  34.0 0.1 pad_add_fusion.meta_ref
  34.1 10.6 %collective-permute-done.halo_ref = bf16[4,2,256,128]{3,2,1,0:T(8,128)(2,1)S(1)} collective-permute-done((bf16[4,2,256,128]{3,2,1,0:T(8,128)(2,1)S(1)}, bf16[4,2,256,128]{3,2,1,0:T(8,128)(2,1)S(1)}, u32[]{:S(2)}, u32[]{:S(2)}) %collective-permute-start) | collective-permute-done | bytes 524320 | tf_op jit(solution)/shard_map/ppermute | solution.py:372
  44.7 1.7 %shard_map.85 = (bf16[24,2,128,128]{3,2,1,0:T(8,128)(2,1)S(1)}, bf16[24,2,128,128]{3,2,1,0:T(8,128)(2,1)S(1)}) custom-call(s32[2]{0:T(128)S(1)} %pad_add_fusion.1.meta_ref, bf16[8,2,256,128]{3,2,1,0:T(8,128)(2,1)S(1)} %all-to-all-done.kv_ref, bf16[4,2,256,128]{3,2,1,0:T(8,128)(2,1)S(1)} %collective-permute-done.halo_ref), custom_call_target="tpu_custom_call" | custom-call | flops 1000000 | bytes 6291456 | tf_op jit(solution)/shard_map/pallas_call | solution.py:71
  46.4 0.0 copy-start
  46.4 1.2 copy-done
  47.6 8.3 %all-to-all-done.1.x_hbm = bf16[8,4,256,128]{3,2,1,0:T(8,128)(2,1)} async-done(((bf16[8,4,256,128]{3,2,1,0:T(8,128)(2,1)}), bf16[8,4,256,128]{3,2,1,0:T(8,128)(2,1)}, u32[]{:S(2)}, u32[]{:S(2)}) %all-to-all-start.1) | async-done | bytes 2097184 | tf_op jit(solution)/shard_map/all_to_all | solution.py:360
  55.9 0.0 copy-start.1
  55.9 1.4 %copy-done.1 = bf16[24,2,128,128]{3,2,1,0:T(8,128)(2,1)S(1)} copy-done((bf16[24,2,128,128]{3,2,1,0:T(8,128)(2,1)S(1)}, bf16[24,2,128,128]{3,2,1,0:T(8,128)(2,1)}, u32[]{:S(2)}) %copy-start.1) | copy-done | bytes 1572888
  57.3 18.2 %shard_map.86 = (bf16[8,4,256,128]{3,2,1,0:T(8,128)(2,1)}, f32[8,2,256,128]{3,2,1,0:T(8,128)}, bf16[4,2,256,128]{3,2,1,0:T(8,128)(2,1)S(1)}) custom-call(s32[18]{0:T(128)S(1)} %pad_add_fusion.meta_ref, s32[32,1]{1,0:T(8,128)S(1)} %copy.16.ends_ref, bf16[24,2,128,128]{3,2,1,0:T(8,128)(2,1)S(1)} %get-tuple-element.13.k_hbm, ...), custom_call_target="tpu_custom_call" | custom-call | flops 5000000000 | bytes 12582912 | tf_op jit(solution)/shard_map/pallas_call | solution.py:266
  75.5 6.3 %all-to-all-start.2 = ((bf16[8,4,256,128]{3,2,1,0:T(8,128)(2,1)}), bf16[8,4,256,128]{3,2,1,0:T(8,128)(2,1)S(1)}, u32[]{:S(2)}, u32[]{:S(2)}) async-start(bf16[8,4,256,128]{3,2,1,0:T(8,128)(2,1)} %get-tuple-element.16), calls=%async_computation.2 | async-start | bytes 4194304 | tf_op jit(solution)/shard_map/all_to_all | solution.py:360
  81.9 1.3 collective-permute-start.1
  83.2 14.1 %collective-permute-done.1 = bf16[4,2,256,128]{3,2,1,0:T(8,128)(2,1)S(1)} collective-permute-done((bf16[4,2,256,128]{3,2,1,0:T(8,128)(2,1)S(1)}, bf16[4,2,256,128]{3,2,1,0:T(8,128)(2,1)S(1)}, u32[]{:S(2)}, u32[]{:S(2)}) %collective-permute-start.1) | collective-permute-done | bytes 524320 | tf_op jit(solution)/shard_map/ppermute | solution.py:377
  97.2 2.9 %add_convert_fusion = bf16[8,2,256,128]{3,2,1,0:T(8,128)(2,1)} fusion(f32[8,2,256,128]{3,2,1,0:T(8,128)} %get-tuple-element.17, bf16[4,2,256,128]{3,2,1,0:T(8,128)(2,1)S(1)} %collective-permute-done.1, f32[2]{0:T(128)S(1)} %compare_select_fusion), kind=kLoop, calls=%fused_computation.1 | loop fusion | flops 2097152 | bytes 3670024 | tf_op jit(solution)/shard_map/convert_element_type | solution.py:381
  100.1 7.6 %all-to-all-done.2 = bf16[8,4,256,128]{3,2,1,0:T(8,128)(2,1)S(1)} async-done(((bf16[8,4,256,128]{3,2,1,0:T(8,128)(2,1)}), bf16[8,4,256,128]{3,2,1,0:T(8,128)(2,1)S(1)}, u32[]{:S(2)}, u32[]{:S(2)}) %all-to-all-start.2) | async-done | bytes 2097184 | tf_op jit(solution)/shard_map/all_to_all | solution.py:360
  107.7 4.2 %all-to-all-start.3 = ((bf16[8,2,256,128]{3,2,1,0:T(8,128)(2,1)}), bf16[8,2,256,128]{3,2,1,0:T(8,128)(2,1)}, u32[]{:S(2)}, u32[]{:S(2)}) async-start(bf16[8,2,256,128]{3,2,1,0:T(8,128)(2,1)} %add_convert_fusion), calls=%async_computation.3 | async-start | bytes 2097152 | tf_op jit(solution)/shard_map/all_to_all | solution.py:360
  111.9 0.2 fusion
  112.1 2.7 %copy_bitcast_fusion = (bf16[256,16,128]{2,1,0:T(8,128)(2,1)}, bf16[256,16,128]{2,1,0:T(8,128)(2,1)}) fusion(bf16[16,256,128]{2,1,0:T(8,128)(2,1)S(1)} %bitcast.15, bf16[16,256,128]{2,1,0:T(8,128)(2,1)S(1)} %bitcast.16), kind=kLoop, calls=%fused_computation.2 | loop fusion | bytes 4194304 | tf_op jit(solution)/shard_map/transpose | solution.py:368
  114.8 13.0 %all-to-all-done.3.x_ref = bf16[8,2,256,128]{3,2,1,0:T(8,128)(2,1)} async-done(((bf16[8,2,256,128]{3,2,1,0:T(8,128)(2,1)}), bf16[8,2,256,128]{3,2,1,0:T(8,128)(2,1)}, u32[]{:S(2)}, u32[]{:S(2)}) %all-to-all-start.3) | async-done | bytes 1048608 | tf_op jit(solution)/shard_map/all_to_all | solution.py:360
  127.8 2.0 %shard_map.87 = (bf16[256,8,128]{2,1,0:T(8,128)(2,1)}, bf16[256,8,128]{2,1,0:T(8,128)(2,1)}) custom-call(bf16[8,2,256,128]{3,2,1,0:T(8,128)(2,1)} %all-to-all-done.3.x_ref), custom_call_target="tpu_custom_call" | custom-call | flops 1000000 | bytes 2097152 | tf_op jit(solution)/shard_map/pallas_call | solution.py:321
  (4 shorter events, 0.1 us)
Async XLA Ops:
  0.6 8.1 %copy-start.2 = (bf16[256,16,128]{2,1,0:T(8,128)(2,1)S(1)}, bf16[256,16,128]{2,1,0:T(8,128)(2,1)}, u32[]{:S(2)}) copy-start(bf16[256,16,128]{2,1,0:T(8,128)(2,1)} %param.5) | copy-start | bytes 3145732
  2.8 6.2 %copy-start.3 = (bf16[256,16,128]{2,1,0:T(8,128)(2,1)S(1)}, bf16[256,16,128]{2,1,0:T(8,128)(2,1)}, u32[]{:S(2)}) copy-start(bf16[256,16,128]{2,1,0:T(8,128)(2,1)} %param.8) | copy-start | bytes 3145732
  2.8 21.7 %all-to-all-start = ((bf16[8,2,256,128]{3,2,1,0:T(8,128)(2,1)}), bf16[8,2,256,128]{3,2,1,0:T(8,128)(2,1)S(1)}, u32[]{:S(2)}, u32[]{:S(2)}) async-start(bf16[8,2,256,128]{3,2,1,0:T(8,128)(2,1)} %shard_map.84), calls=%async_computation | async-start | bytes 2097152 | tf_op jit(solution)/shard_map/all_to_all | solution.py:360
  10.8 18.0 %copy-start.4 = (s32[32]{0:T(128)S(1)}, s32[32]{0:T(128)}, u32[]{:S(2)}) copy-start(s32[32]{0:T(128)} %param.9) | copy-start | bytes 388
  24.5 31.4 %all-to-all-start.1 = ((bf16[8,4,256,128]{3,2,1,0:T(8,128)(2,1)}), bf16[8,4,256,128]{3,2,1,0:T(8,128)(2,1)}, u32[]{:S(2)}, u32[]{:S(2)}) async-start(bf16[8,4,256,128]{3,2,1,0:T(8,128)(2,1)} %pad_maximum_fusion), calls=%async_computation.1 | async-start | bytes 4194304 | tf_op jit(solution)/shard_map/all_to_all | solution.py:360
  29.1 15.6 %collective-permute-start = (bf16[4,2,256,128]{3,2,1,0:T(8,128)(2,1)S(1)}, bf16[4,2,256,128]{3,2,1,0:T(8,128)(2,1)S(1)}, u32[]{:S(2)}, u32[]{:S(2)}) collective-permute-start(bf16[4,2,256,128]{3,2,1,0:T(8,128)(2,1)S(1)} %slice.12), channel_id=1, source_target_pairs={{0,24},{2,26},{4,28},{6,30},{8,16},{10,18},{12,20},{14,22},{1,25},... | collective-permute-start | bytes 1572872 | tf_op jit(solution)/shard_map/ppermute | solution.py:372
  46.4 1.2 copy-start
  55.9 1.4 %copy-start.1 = (bf16[24,2,128,128]{3,2,1,0:T(8,128)(2,1)S(1)}, bf16[24,2,128,128]{3,2,1,0:T(8,128)(2,1)}, u32[]{:S(2)}) copy-start(bf16[24,2,128,128]{3,2,1,0:T(8,128)(2,1)} %copy-done) | copy-start | bytes 4718596
  75.5 32.2 %all-to-all-start.2 = ((bf16[8,4,256,128]{3,2,1,0:T(8,128)(2,1)}), bf16[8,4,256,128]{3,2,1,0:T(8,128)(2,1)S(1)}, u32[]{:S(2)}, u32[]{:S(2)}) async-start(bf16[8,4,256,128]{3,2,1,0:T(8,128)(2,1)} %get-tuple-element.16), calls=%async_computation.2 | async-start | bytes 4194304 | tf_op jit(solution)/shard_map/all_to_all | solution.py:360
  81.9 15.4 %collective-permute-start.1 = (bf16[4,2,256,128]{3,2,1,0:T(8,128)(2,1)S(1)}, bf16[4,2,256,128]{3,2,1,0:T(8,128)(2,1)S(1)}, u32[]{:S(2)}, u32[]{:S(2)}) collective-permute-start(bf16[4,2,256,128]{3,2,1,0:T(8,128)(2,1)S(1)} %get-tuple-element.18), channel_id=1, source_target_pairs={{24,0},{26,2},{28,4},{30,6},{16,8},{18,10},{20,12},{22,14},{25,1},... | collective-permute-start | bytes 1572872 | tf_op jit(solution)/shard_map/ppermute | solution.py:377
  107.7 20.1 %all-to-all-start.3 = ((bf16[8,2,256,128]{3,2,1,0:T(8,128)(2,1)}), bf16[8,2,256,128]{3,2,1,0:T(8,128)(2,1)}, u32[]{:S(2)}, u32[]{:S(2)}) async-start(bf16[8,2,256,128]{3,2,1,0:T(8,128)(2,1)} %add_convert_fusion), calls=%async_computation.3 | async-start | bytes 2097152 | tf_op jit(solution)/shard_map/all_to_all | solution.py:360
